TPU v7x, 32 devices: a whole 2x2x4 slice. The times are simulated.
32 devices in a mesh: kv: 4 (over z), blk: 8 (over y, x, core).
Axes of the slice: x: 2, y: 2, z: 4, core: 2. Of those that a mesh axis runs over, the one named last changes fastest.
Arguments:
- hidden_in: bfloat16 [4, 16, 4096], P(None, None, 'blk'), may hold values from -6 to 6
- attn_gain: bfloat16 [4096], P('blk'), may hold values from 0.5 to 1.5
- ffn_gain: bfloat16 [4096], replicated, may hold values from 0.5 to 1.5
- query_key_value_weight: bfloat16 [4096, 8, 768], P('blk', 'kv'), may hold values from -0.09375 to 0.09375
- out_weight: bfloat16 [4096, 4096], P('kv', 'blk'), may hold values from -0.09375 to 0.09375
- router_weight: bfloat16 [4096, 8], replicated, may hold values from -0.09375 to 0.09375
- expert_in: bfloat16 [8, 4096, 2, 8192], P('kv', None, None, 'blk'), may hold values from -0.09375 to 0.09375
- expert_down: bfloat16 [8, 8192, 4096], P('kv', 'blk'), may hold values from -0.09375 to 0.09375
- kv_cache: bfloat16 [2048, 2, 8, 128, 128], P('blk', None, 'kv')
- lengths: int32 [2], replicated, may hold values from 1 to 16384, as said below
- tables: int32 [16, 128], replicated, may hold values from 0 to 2047, as said below
- parents: int32 [4, 16], replicated, may hold values from 0 to 15, as said below
- routes: int32 [4, 16, 2], replicated, may hold values from 0 to 7, all different within a row; in each aligned block of 16 rows (0 to 15, 16 to 31, ..., all dimensions but the last counted through in order) at most 6 rows name the same one
Outputs:
- layer_out: bfloat16 [4, 16, 4096], P(None, None, 'blk')
Inputs may be any that keep to these rules, and one draw needn't show every extreme that they name: `lengths`: one group has exactly 16384 cached positions. `tables`: each pool block is named exactly once. `parents`: a beam's parent is a beam of its own group of 8 consecutive beams. `routes`: in each step no expert is named by more than 6 beams, a bound that some block reaches.
All inputs are finite; a program needn't handle non-finite values.
Results may differ from a plain program's by a relative error of at most 0.013.
Values may be sent and summed in bfloat16 or wider, within the bound.
A program may use at most 192 MiB of HBM per device.

v0:
```python
import math

import jax
import jax.numpy as jnp
from jax import lax
from jax.sharding import PartitionSpec as P

MODEL_WIDTH = 4096
HEAD_WIDTH = 128
QUERIES_PER_KEY = 4
EXPERTS = 8
BEAM_W = 8
GROUPS = 2
DECODE_STEPS = 4
BLOCK_POSITIONS = 128
BEAM_BLOCKS = 128
BEAM_TOTAL = 16
CAP = 6


NORM_FLOOR = 1e-05
ROPE_BASE = 1000000.0
NEG_FILL = -1e30


def joined(value, axis, join):
    pieces = jax.tree.map(lambda part: lax.all_gather(part, axis), value)
    head = jax.tree.map(lambda part: part[0], pieces)
    tail = jax.tree.map(lambda part: part[1:], pieces)
    running, _ = lax.scan(lambda running, section: (join(running, section), None), head, tail)
    return running


def rotate_pairs(vectors, positions):
    half_width = vectors.shape[-1] // 2
    exponents = jnp.arange(half_width, dtype=jnp.float32) * (2.0 / vectors.shape[-1])
    frequency = ROPE_BASE ** (-exponents)
    angles = positions.astype(jnp.float32)[..., None] * frequency
    cosine = jnp.cos(angles)
    sine_part = jnp.sin(angles)
    lower_half = vectors[..., :half_width]
    upper_half = vectors[..., half_width:]
    return jnp.concatenate(
        [
            lower_half * cosine - upper_half * sine_part,
            upper_half * cosine + lower_half * sine_part,
        ],
        axis=-1,
    )


def lineage(parents):
    steps_count, beam_count = parents.shape
    beam_ids = jnp.arange(beam_count, dtype=jnp.int32)
    line_rows = []
    anchor_rows = []
    for step_index in range(steps_count):
        current = beam_ids
        levels = [jnp.full((beam_count,), -1, jnp.int32) for level_index in range(steps_count)]
        for level_index in range(step_index, -1, -1):
            levels[level_index] = current
            current = parents[level_index][current]
        line_rows.append(jnp.stack(levels))
        anchor_rows.append(current)
    return (jnp.stack(line_rows), jnp.stack(anchor_rows))


def expert_rank(routes):
    steps_count, beam_count, pick_count = routes.shape
    onehot = (routes[..., None] == jnp.arange(EXPERTS, dtype=jnp.int32)).astype(jnp.int32)
    flat_hits = onehot.reshape(steps_count, beam_count * pick_count, EXPERTS)
    before = jnp.cumsum(flat_hits, axis=1) - flat_hits
    return jnp.sum(before * flat_hits, axis=-1).reshape(steps_count, beam_count, pick_count)


def head_total(partial_value):
    return lax.psum(partial_value, "kv")


def combine_parts(part_one, part_two):
    max_one, sum_one, vector_one = part_one
    max_two, sum_two, vector_two = part_two
    larger = jnp.maximum(max_one, max_two)
    scale_one = jnp.exp(max_one - larger)
    scale_two = jnp.exp(max_two - larger)
    return (
        larger,
        sum_one * scale_one + sum_two * scale_two,
        vector_one * scale_one[..., None] + vector_two * scale_two[..., None],
    )


def groups_to_beams(grouped):
    shaped = grouped.reshape((GROUPS, DECODE_STEPS, BEAM_W, QUERIES_PER_KEY) + grouped.shape[2:])
    shaped = jnp.moveaxis(shaped, 1, 0)
    return shaped.reshape((DECODE_STEPS, BEAM_TOTAL, QUERIES_PER_KEY) + grouped.shape[2:])


def body(
    hidden_in,
    attn_gain,
    ffn_gain,
    query_key_value_weight,
    out_weight,
    router_weight,
    expert_in,
    expert_down,
    kv_cache,
    lengths,
    tables,
    parents,
    routes,
):
    count_tokens = DECODE_STEPS * BEAM_TOTAL
    width_local = hidden_in.shape[2]
    heads_local = query_key_value_weight.shape[1]
    logit_scale = 1.0 / math.sqrt(HEAD_WIDTH)
    line_beams, anchor = lineage(parents)
    flat_in = hidden_in.reshape(count_tokens, width_local).astype(jnp.float32)
    pre_attn = (flat_in * attn_gain.astype(jnp.float32)).astype(jnp.bfloat16)
    partial_proj = jnp.dot(
        pre_attn,
        query_key_value_weight.reshape(width_local, -1),
        preferred_element_type=jnp.float32,
    )
    partial_sq = jnp.sum(flat_in * flat_in, axis=1)
    projected_rows, square_sum = lax.psum((partial_proj, partial_sq), "blk")
    projected_rows = (
        projected_rows * lax.rsqrt(square_sum / MODEL_WIDTH + NORM_FLOOR)[:, None]
    ).reshape(DECODE_STEPS, BEAM_TOTAL, heads_local, QUERIES_PER_KEY + 2, HEAD_WIDTH)
    beam_groups = jnp.arange(BEAM_TOTAL, dtype=jnp.int32) // BEAM_W
    positions = lengths[beam_groups][None, :] + jnp.arange(DECODE_STEPS, dtype=jnp.int32)[:, None]
    queries = rotate_pairs(
        projected_rows[:, :, :, :QUERIES_PER_KEY], positions[:, :, None, None]
    ).astype(jnp.bfloat16)
    new_key = rotate_pairs(projected_rows[:, :, :, QUERIES_PER_KEY], positions[:, :, None]).astype(
        jnp.bfloat16
    )
    new_value = projected_rows[:, :, :, QUERIES_PER_KEY + 1].astype(jnp.bfloat16)
    slot_count = kv_cache.shape[0]
    slot_base = lax.axis_index("blk") * slot_count
    entry_ids = jnp.arange(BEAM_TOTAL * BEAM_BLOCKS, dtype=jnp.int32)
    owner_all = (
        jnp.zeros((BEAM_TOTAL * BEAM_BLOCKS,), jnp.int32)
        .at[tables.reshape(-1)]
        .set(entry_ids // BEAM_BLOCKS)
    )
    block_all = (
        jnp.zeros((BEAM_TOTAL * BEAM_BLOCKS,), jnp.int32)
        .at[tables.reshape(-1)]
        .set(entry_ids % BEAM_BLOCKS)
    )
    owner_here = lax.dynamic_slice_in_dim(owner_all, slot_base, slot_count)
    block_here = lax.dynamic_slice_in_dim(block_all, slot_base, slot_count)
    group_here = owner_here // BEAM_W
    live_keys = (
        block_here[:, None] * BLOCK_POSITIONS
        + jnp.arange(BLOCK_POSITIONS, dtype=jnp.int32)[None, :]
        < lengths[group_here][:, None]
    )
    anchor_groups = jnp.moveaxis(anchor.reshape(DECODE_STEPS, GROUPS, BEAM_W), 1, 0)
    anchor_query = jnp.broadcast_to(
        anchor_groups[..., None], (GROUPS, DECODE_STEPS, BEAM_W, QUERIES_PER_KEY)
    ).reshape(GROUPS, -1)
    query_match = anchor_query[group_here] == owner_here[:, None]
    group_hits = group_here[:, None] == jnp.arange(GROUPS, dtype=jnp.int32)[None, :]
    group_float = group_hits.astype(jnp.float32)
    recent_allowed = jnp.transpose(
        line_beams[:, :, :, None] == jnp.arange(BEAM_TOTAL, dtype=jnp.int32), (0, 2, 1, 3)
    ).reshape(DECODE_STEPS, BEAM_TOTAL, 1, count_tokens)
    is_first = lax.axis_index("blk") == 0
    max_heads = []
    sum_heads = []
    vector_heads = []
    for head_index in range(heads_local):
        query_head = queries[:, :, head_index]
        query_groups = jnp.moveaxis(
            query_head.reshape(DECODE_STEPS, GROUPS, BEAM_W, QUERIES_PER_KEY, HEAD_WIDTH), 1, 0
        ).reshape(GROUPS, -1, HEAD_WIDTH)
        query_slots = query_groups[group_here]
        key_matrix = kv_cache[:, 0, head_index]
        value_matrix = kv_cache[:, 1, head_index]
        scores = (
            jnp.einsum("ptd,pqd->ptq", key_matrix, query_slots, preferred_element_type=jnp.float32)
            * logit_scale
        )
        allowed = live_keys[:, :, None] & query_match[:, None, :]
        masked = jnp.where(allowed, scores, NEG_FILL)
        slot_max = jnp.max(masked, axis=1)
        weights = jnp.where(allowed, jnp.exp(masked - slot_max[:, None, :]), 0.0)
        slot_sum = jnp.sum(weights, axis=1)
        slot_vector = jnp.einsum(
            "ptq,ptd->pqd",
            weights.astype(jnp.bfloat16),
            value_matrix,
            preferred_element_type=jnp.float32,
        )
        group_max = jnp.max(
            jnp.where(group_hits[:, :, None], slot_max[:, None, :], NEG_FILL), axis=0
        )
        rescale = jnp.exp(slot_max - group_max[group_here])
        group_sum = jnp.einsum(
            "pg,pq->gq", group_float, slot_sum * rescale, precision=lax.Precision.HIGHEST
        )
        group_vector = jnp.einsum(
            "pg,pqd->gqd",
            group_float,
            slot_vector * rescale[:, :, None],
            precision=lax.Precision.HIGHEST,
        )
        cache_max = groups_to_beams(group_max)
        cache_sum = groups_to_beams(group_sum)
        cache_vector = groups_to_beams(group_vector)
        newest_keys = new_key[:, :, head_index].reshape(count_tokens, HEAD_WIDTH)
        newest_values = new_value[:, :, head_index].reshape(count_tokens, HEAD_WIDTH)
        newest_logits = (
            jnp.einsum("sbqd,kd->sbqk", query_head, newest_keys, preferred_element_type=jnp.float32)
            * logit_scale
        )
        recent_masked = jnp.where(recent_allowed, newest_logits, NEG_FILL)
        recent_max = jnp.max(recent_masked, axis=-1)
        recent_weights = jnp.where(
            recent_allowed, jnp.exp(recent_masked - recent_max[..., None]), 0.0
        )
        recent_sum = jnp.sum(recent_weights, axis=-1)
        recent_vector = jnp.einsum(
            "sbqk,kd->sbqd",
            recent_weights.astype(jnp.bfloat16),
            newest_values,
            preferred_element_type=jnp.float32,
        )
        recent_max = jnp.where(is_first, recent_max, NEG_FILL)
        recent_sum = jnp.where(is_first, recent_sum, 0.0)
        recent_vector = jnp.where(is_first, recent_vector, 0.0)
        local_max, local_sum, local_vector = combine_parts(
            (cache_max, cache_sum, cache_vector), (recent_max, recent_sum, recent_vector)
        )
        max_heads.append(local_max)
        sum_heads.append(local_sum)
        vector_heads.append(local_vector)
    part_max = jnp.stack(max_heads, axis=2)
    part_sum = jnp.stack(sum_heads, axis=2)
    part_vector = jnp.stack(vector_heads, axis=2)
    whole_max, whole_sum, whole_vector = joined(
        (part_max, part_sum, part_vector), "blk", combine_parts
    )
    attended_rows = (
        (whole_vector / whole_sum[..., None]).astype(jnp.bfloat16).reshape(count_tokens, -1)
    )
    attn_partial = jnp.dot(attended_rows, out_weight, preferred_element_type=jnp.float32)
    attn_out = head_total(attn_partial)
    residual = (flat_in + attn_out).astype(jnp.bfloat16)
    experts_local = expert_in.shape[0]
    ff_local = expert_in.shape[3]
    rows_per_expert = DECODE_STEPS * CAP
    rows_local = experts_local * rows_per_expert
    flat_routes = routes.reshape(count_tokens, 2)
    rank = expert_rank(routes).reshape(count_tokens, 2)
    step_of = jnp.arange(count_tokens, dtype=jnp.int32) // BEAM_TOTAL
    row_id = (flat_routes * rows_per_expert + step_of[:, None] * CAP + rank).reshape(-1)
    token_ids = jnp.broadcast_to(
        jnp.arange(count_tokens, dtype=jnp.int32)[:, None], (count_tokens, 2)
    ).reshape(-1)
    table_size = EXPERTS * rows_per_expert
    row_token_all = jnp.zeros((table_size,), jnp.int32).at[row_id].set(token_ids)
    row_live_all = jnp.zeros((table_size,), jnp.float32).at[row_id].set(1.0)
    row_other_all = (
        jnp.zeros((table_size,), jnp.int32).at[row_id].set(flat_routes[:, ::-1].reshape(-1))
    )
    row_start = lax.axis_index("kv") * rows_local
    row_token = lax.dynamic_slice_in_dim(row_token_all, row_start, rows_local)
    row_live = lax.dynamic_slice_in_dim(row_live_all, row_start, rows_local)
    row_other = lax.dynamic_slice_in_dim(row_other_all, row_start, rows_local)
    row_own = (row_start + jnp.arange(rows_local, dtype=jnp.int32)) // rows_per_expert
    in_flat = expert_in.reshape(experts_local, MODEL_WIDTH, 2 * ff_local)
    gain_wide = ffn_gain.astype(jnp.float32)
    full_rows = lax.all_gather(residual, "blk", axis=1, tiled=True)
    chosen = full_rows[row_token].astype(jnp.float32)
    pre_rows = (chosen * gain_wide).astype(jnp.bfloat16)
    sums_in = jnp.einsum(
        "erd,edf->erf",
        pre_rows.reshape(experts_local, rows_per_expert, MODEL_WIDTH),
        in_flat,
        preferred_element_type=jnp.float32,
    )
    sums_router = jnp.dot(pre_rows, router_weight, preferred_element_type=jnp.float32)
    sum_sq = jnp.sum(chosen * chosen, axis=1)
    inv_rows = lax.rsqrt(sum_sq / MODEL_WIDTH + NORM_FLOOR)
    expert_act = sums_in * inv_rows.reshape(experts_local, rows_per_expert)[:, :, None]
    expert_hidden = (jax.nn.silu(expert_act[..., :ff_local]) * expert_act[..., ff_local:]).astype(
        jnp.bfloat16
    )
    down_part = jnp.einsum(
        "erf,efd->erd", expert_hidden, expert_down, preferred_element_type=jnp.float32
    ).reshape(rows_local, MODEL_WIDTH)
    expert_result = lax.psum_scatter(down_part, "blk", scatter_dimension=1, tiled=True)
    logits = sums_router * inv_rows[:, None]
    expert_ids = jnp.arange(EXPERTS, dtype=jnp.int32)
    own_logit = jnp.sum(jnp.where(row_own[:, None] == expert_ids[None, :], logits, 0.0), axis=1)
    other_logit = jnp.sum(jnp.where(row_other[:, None] == expert_ids[None, :], logits, 0.0), axis=1)
    gate_share = row_live / (1.0 + jnp.exp(other_logit - own_logit))
    weighted_values = expert_result * gate_share[:, None]
    placement = (row_token[None, :] == jnp.arange(count_tokens, dtype=jnp.int32)[:, None]).astype(
        jnp.float32
    )
    mixture_part = jnp.dot(placement, weighted_values, precision=lax.Precision.HIGHEST)
    mixture = head_total(mixture_part)
    layer_out = (residual.astype(jnp.float32) + mixture).astype(jnp.bfloat16)
    return layer_out.reshape(DECODE_STEPS, BEAM_TOTAL, width_local)


def solution(mesh):
    placed = (
        P(None, None, "blk"),
        P("blk"),
        P(),
        P("blk", "kv", None),
        P("kv", "blk"),
        P(),
        P("kv", None, None, "blk"),
        P("kv", "blk", None),
        P("blk", None, "kv", None, None),
        P(),
        P(),
        P(),
        P(),
    )
    return jax.shard_map(
        body, mesh=mesh, in_specs=placed, out_specs=P(None, None, "blk"), check_vma=False
    )
```

profile of v0, /device:TPU:0, one launch (start us, length us, event | category | flops | bytes accessed | tf_op | source)
XLA Modules:
  0.0 417.6 jit_solution(14028096900187270121)
XLA Ops:
  7.3 1.7 copy.167
  9.0 0.9 multiply_reduce_fusion.1
  9.9 1.1 fusion.133
  11.2 1.3 fusion.129
  13.2 8.0 %scatter_custom_fusion = s32[2048]{0:T(1024)S(1)} fusion(s32[2048]{0:T(1024)S(1)} %bitcast.306, s32[2048]{0:T(1024)S(1)} %add_select_fusion, s32[]{:T(128)} %constant.128.clone.1), kind=kCustom, calls=%fused_computation.202 | custom fusion | bytes 8196 | tf_op jit(solution)/shard_map/scatter | solution.py:146
  21.3 8.0 %scatter_custom_fusion.1 = s32[2048]{0:T(1024)S(1)} fusion(s32[2048]{0:T(1024)S(1)} %bitcast.307, s32[2048]{0:T(1024)S(1)} %fusion.79, s32[]{:T(128)} %constant.128.clone.1), kind=kCustom, calls=%fused_computation.200 | custom fusion | bytes 8196 | tf_op jit(solution)/shard_map/scatter | solution.py:151
  29.3 1.3 fusion.100
  30.6 1.4 compare_select_fusion.12
  32.7 0.8 copy.146
  33.6 0.8 slice_bitcast_fusion
  43.2 15.1 %psum.29 = f32[64]{0:T(128)S(1)} all-reduce(f32[64]{0:T(128)S(1)} %reduce_sum.84), channel_id=1, replica_groups=mesh['kv'=4,'blk'=8] {'blk'}, use_global_device_ids=true, to_apply=%region_4.5 | all-reduce | flops 64 | bytes 512 | tf_op jit(solution)/shard_map/psum | solution.py:127
  59.0 2.0 scatter_custom_fusion.2
  61.8 6.3 %all-reduce.4.cloned.1.call-done = f32[64,1536]{1,0:T(8,128)} async-done(((f32[64,1536]{1,0:T(8,128)}), f32[64,1536]{1,0:T(8,128)}) %all-reduce.4.cloned.1.call-update) | async-done | bytes 393232 | tf_op jit(solution)/shard_map/psum | solution.py:127
  68.1 1.1 broadcast_multiply_fusion
  70.0 8.4 %gather_fusion.12 = bf16[256,128,128]{2,1,0:T(8,128)(2,1)} fusion(bf16[2,128,128]{2,1,0:T(8,128)(2,1)S(1)} %bitcast.280, s32[1024]{0:T(1024)S(1)} %pad_clamp_fusion.1), kind=kCustom, calls=%fused_computation.12 | custom fusion | bytes 16778240 | tf_op jit(solution)/shard_map/gather | solution.py:180
  78.4 8.4 %gather_fusion.11 = bf16[256,128,128]{2,1,0:T(8,128)(2,1)} fusion(bf16[2,128,128]{2,1,0:T(8,128)(2,1)S(1)} %bitcast.279, s32[1024]{0:T(1024)S(1)} %pad_clamp_fusion.1), kind=kCustom, calls=%fused_computation.11 | custom fusion | bytes 16778240 | tf_op jit(solution)/shard_map/gather | solution.py:180
  86.8 12.8 %fusion.19 = f32[256,128,128]{1,2,0:T(8,128)} fusion(bf16[256,128,128]{2,1,0:T(8,128)(2,1)} %gather_fusion.12, bf16[256,2,2,128,128]{4,3,2,1,0:T(8,128)(2,1)} %param.23), kind=kOutput, calls=%fused_computation.52 | convolution fusion | flops 1073741824 | bytes 33554432 | tf_op jit(solution)/shard_map/ptd,pqd->ptq/dot_general | solution.py:184
  99.6 20.5 %fusion.9 = (f32[256,128]{1,0:T(8,128)S(1)}, f32[256,128]{1,0:T(8,128)S(1)}, f32[256,128,128]{1,2,0:T(8,128)}) fusion(pred[256,128]{1,0:T(8,128)(4,1)S(1)} %broadcast_compare_fusion, pred[256,128]{1,0:T(8,128)(4,1)S(1)} %add_compare_fusion, f32[256,128,128]{1,2,0:T(8,128)} %fusion.19, bf16[256,128,128]{2,1,0:T(8,128)(2,1)} %gather_fusion.11, ...), kind=kOutput, calls=%fused_computation.42 | convolution fusion | flops 1103036416 | bytes 50659328 | tf_op jit(solution)/shard_map/ptd,pqd->ptq/dot_general | solution.py:184
  123.6 19.6 %convolution_multiply_fusion = f32[256,128,128]{2,1,0:T(8,128)} fusion(f32[256,128,128]{1,2,0:T(8,128)} %fusion.19, f32[256,128]{1,0:T(8,128)S(1)} %subtract_exponential_fusion.2, bf16[256,2,2,128,128]{4,3,2,1,0:T(8,128)(2,1)} %param.23, f32[256,128]{1,0:T(8,128)S(1)} %get-tuple-element.76, pred[256,128]{1,0:T(8,128)(4,1)S(1)} %broadcast_compare_fusion, ...), kind=kOutput, calls=%fused_computation.48 | convolution fusion | flops 1103101952 | bytes 42270720 | tf_op jit(solution)/shard_map/ptq,ptd->pqd/dot_general | solution.py:192
  143.2 20.0 %fusion.5 = f32[2,128,128]{2,0,1:T(2,128)S(1)} fusion(f32[256,128,128]{2,1,0:T(8,128)} %convolution_multiply_fusion, s32[256]{0:T(256)S(1)} %get-tuple-element.104), kind=kOutput, calls=%fused_computation.38 | convolution fusion | flops 100663808 | bytes 16909312 | tf_op jit(solution)/shard_map/pg,pqd->gqd/dot_general | solution.py:205
  163.3 18.7 %convolution_multiply_fusion.1 = f32[256,128,128]{2,1,0:T(8,128)} fusion(f32[256,128,128]{1,2,0:T(8,128)S(1)} %bitcast.282, f32[256,128]{1,0:T(8,128)S(1)} %subtract_exponential_fusion.3, bf16[256,2,2,128,128]{4,3,2,1,0:T(8,128)(2,1)} %param.23, f32[256,128]{1,0:T(8,128)S(1)} %get-tuple-element.75, pred[256,128]{1,0:T(8,128)(4,1)S(1)} %broadcast_compare_fusion, ...), kind=kOutput, calls=%fused_computation.49 | convolution fusion | flops 1103101952 | bytes 42270720 | tf_op jit(solution)/shard_map/ptq,ptd->pqd/dot_general | solution.py:192
  182.0 20.0 %fusion.7 = f32[2,128,128]{2,0,1:T(2,128)S(1)} fusion(f32[256,128,128]{2,1,0:T(8,128)} %convolution_multiply_fusion.1, s32[256]{0:T(256)S(1)} %get-tuple-element.104), kind=kOutput, calls=%fused_computation.40 | convolution fusion | flops 100663808 | bytes 16909312 | tf_op jit(solution)/shard_map/pg,pqd->gqd/dot_general | solution.py:205
  203.4 13.5 %fusion.12 = (f32[256,128]{1,0:T(8,128)S(1)}, f32[256,128]{1,0:T(8,128)S(1)}) fusion(f32[256,128,128]{1,2,0:T(8,128)} %get-tuple-element.145, f32[256,128]{1,0:T(8,128)S(1)} %get-tuple-element.75, pred[256,128]{1,0:T(8,128)(4,1)S(1)} %broadcast_compare_fusion, pred[256,128]{1,0:T(8,128)(4,1)S(1)} %add_compare_fusion, f32[256,128]{1,0:T(8,128)S(1)} %get-tuple-element.76, ...), kind=kLoop, calls=%fused_computation.45 | loop fusion | flops 46071808 | bytes 34144256 | tf_op jit(solution)/shard_map/reduce_sum | solution.py:191
  218.2 8.7 %all-gather = f32[32,16,2,4]{1,3,0,2:T(4,128)S(1)} all-gather(f32[4,16,2,4]{1,3,0,2:T(4,128)S(1)} %pad_maximum_fusion.3), channel_id=2, replica_groups=mesh['kv'=4,'blk'=8] {'blk'}, dimensions={0}, use_global_device_ids=true | all-gather | bytes 18432 | tf_op jit(solution)/shard_map/all_gather | solution.py:27
  227.0 9.2 %all-gather.1 = f32[32,16,2,4]{1,3,0,2:T(4,128)S(1)} all-gather(f32[4,16,2,4]{1,3,0,2:T(4,128)S(1)} %pad_maximum_fusion.4), channel_id=3, replica_groups=mesh['kv'=4,'blk'=8] {'blk'}, dimensions={0}, use_global_device_ids=true | all-gather | bytes 18432 | tf_op jit(solution)/shard_map/all_gather | solution.py:27
  236.2 1.0 slice.180
  237.3 1.6 slice.183
  239.0 8.0 %while.14 = (s32[]{:T(128)}, f32[4,16,2,4]{1,3,2,0:T(4,128)S(1)}, f32[4,16,2,4]{1,3,2,0:T(4,128)S(1)}, f32[4,16,2,4,128]{4,3,2,1,0:T(4,128)S(1)}, f32[7,4,16,2,4...) while((s32[]{:T(128)}, f32[4,16,2,4]{1,3,2,0:T(4,128)S(1)}, ...), condition=%wide.region_16.17_spmd, body=%wide.region_15.16_spmd.sunk | while | flops 199682 | bytes 1347685 | solution.py:30
  239.3 0.8 fusion.163
  240.5 0.8 fusion.163
  241.6 0.8 fusion.163
  242.7 0.8 fusion.163
  243.9 0.8 fusion.163
  245.0 0.8 fusion.163
  246.2 0.8 fusion.163
  247.4 0.9 fusion.134
  249.9 54.3 %reshape.744 = bf16[2,4096,2048]{2,1,0:T(8,128)(2,1)} reshape(bf16[2,4096,2,1024]{3,2,1,0:T(2,128)(2,1)} %param.21) | data formatting | bytes 67108864 | tf_op jit(solution)/shard_map/reshape | solution.py:275
  304.2 0.9 fusion.51
  305.1 9.2 %all_gather.27 = bf16[64,4096]{1,0:T(8,128)(2,1)S(1)} all-gather(bf16[64,512]{1,0:T(8,128)(2,1)S(1)} %fusion.51), channel_id=1, replica_groups=mesh['kv'=4,'blk'=8] {'blk'}, dimensions={1}, use_global_device_ids=true | all-gather | bytes 589824 | tf_op jit(solution)/shard_map/all_gather | solution.py:277
  314.3 0.8 gather_fusion.15
  315.4 12.8 %convolution_multiply_fusion.2 = f32[2,24,2048]{2,1,0:T(8,128)S(1)} fusion(bf16[2,4096,2048]{2,1,0:T(8,128)(2,1)} %reshape.744, f32[4096]{0:T(1024)S(1)} %convert_element_type.110, f32[2,24]{1,0:T(2,128)S(1)} %rsqrt.19, bf16[2,24,4096]{2,1,0:T(8,128)(2,1)S(1)} %bitcast.283), kind=kOutput, calls=%fused_computation.72 | convolution fusion | flops 805994496 | bytes 34357440 | tf_op jit(solution)/shard_map/erd,edf->erf/dot_general | solution.py:280
  328.3 9.0 %fusion.60 = f32[2,24,4096]{2,1,0:T(8,128)} fusion(bf16[2,1024,4096]{2,1,0:T(8,128)(2,1)} %param.22, f32[2,24,2048]{2,1,0:T(8,128)S(1)} %convolution_multiply_fusion.2), kind=kOutput, calls=%fused_computation.123 | convolution fusion | flops 402948096 | bytes 17956864 | tf_op jit(solution)/shard_map/erf,efd->erd/dot_general | solution.py:293
  337.7 1.1 scatter_custom_fusion.4
  338.9 1.1 scatter_custom_fusion.3
  340.3 32.1 %reduce-scatter.2.cloned.1.call-done = f32[48,512]{1,0:T(8,128)} async-done(((f32[48,4096]{1,0:T(8,128)}), f32[48,512]{1,0:T(8,128)}) %reduce-scatter.2.cloned.1.call-update) | async-done | bytes 98320 | tf_op jit(solution)/shard_map/reduce_scatter | solution.py:296
  372.4 1.8 fusion.62
  374.2 34.9 %all-reduce.8.cloned.1.call-done = f32[64,512]{1,0:T(8,128)} async-done(((f32[64,512]{1,0:T(8,128)}), f32[64,512]{1,0:T(8,128)}) %all-reduce.8.cloned.1.call-update) | async-done | bytes 131088 | tf_op jit(solution)/shard_map/psum | solution.py:77
  409.1 1.5 add_convert_fusion.1
  (215 shorter events, 24.7 us)
Async XLA Ops:
  6.5 240.8 %copy-start = (bf16[1024,512]{1,0:T(8,128)(2,1)S(1)}, bf16[1024,512]{1,0:T(8,128)(2,1)}, u32[]{:S(2)}) copy-start(bf16[1024,512]{1,0:T(8,128)(2,1)} %param.19) | copy-start | bytes 3145732
  6.5 61.6 %all-reduce.4.cloned.1.call-start = ((), (), s32[]{:S(2)}) async-start(), calls=%async_computation.1 | async-start | bytes 786432 | tf_op jit(solution)/shard_map/psum | solution.py:127
  11.1 225.1 %all-gather.5.cloned.1.call-start = ((), (), s32[]{:S(2)}) async-start(), calls=%async_computation.5 | async-start | bytes 2359296 | tf_op jit(solution)/shard_map/all_gather | solution.py:27
  59.0 27.9 %copy-start.3 = (s32[128]{0:T(128)}, s32[128]{0:T(128)S(1)}, u32[]{:S(2)}) copy-start(s32[128]{0:T(128)S(1)} %fusion.108) | copy-start | bytes 1540
  123.3 40.0 %slice-start = ((s8[16777216]{0:T(1024)(128)(4,1)}), s8[4194304]{0:T(1024)(128)(4,1)S(1)}, s32[]{:S(2)}) async-start(s8[16777216]{0:T(1024)(128)(4,1)} %bitcast.281), calls=%async_computation.6 | async-start | bytes 8388608
  123.6 39.7 %slice-start.1 = ((s8[16777216]{0:T(1024)(128)(4,1)}), s8[4194304]{0:T(1024)(128)(4,1)S(1)}, s32[]{:S(2)}) async-start(s8[16777216]{0:T(1024)(128)(4,1)} %bitcast.281), calls=%async_computation.7 | async-start | bytes 8388608
  123.6 39.7 %slice-start.2 = ((s8[16777216]{0:T(1024)(128)(4,1)}), s8[4194304]{0:T(1024)(128)(4,1)S(1)}, s32[]{:S(2)}) async-start(s8[16777216]{0:T(1024)(128)(4,1)} %bitcast.281), calls=%async_computation.8 | async-start | bytes 8388608
  123.6 39.7 %slice-start.3 = ((s8[16777216]{0:T(1024)(128)(4,1)}), s8[4194304]{0:T(1024)(128)(4,1)S(1)}, s32[]{:S(2)}) async-start(s8[16777216]{0:T(1024)(128)(4,1)} %bitcast.281), calls=%async_computation.9 | async-start | bytes 8388608
  203.3 100.9 %all-reduce.6.cloned.1.call-start = ((), (), s32[]{:S(2)}) async-start(), calls=%async_computation.2 | async-start | bytes 262144 | tf_op jit(solution)/shard_map/psum | solution.py:77
  248.4 124.0 %reduce-scatter.2.cloned.1.call-start = ((), (), s32[]{:S(2)}) async-start(), calls=%async_computation.3 | async-start | bytes 884736 | tf_op jit(solution)/shard_map/reduce_scatter | solution.py:296
  249.9 54.3 %copy-start.1 = (bf16[4,16,512]{2,1,0:T(8,128)(2,1)S(1)}, bf16[4,16,512]{2,1,0:T(8,128)(2,1)}, u32[]{:S(2)}) copy-start(bf16[4,16,512]{2,1,0:T(8,128)(2,1)} %param.15) | copy-start | bytes 196612
  328.2 9.1 %copy-start.2 = (s32[4,16,2]{1,2,0:T(2,128)S(1)}, s32[4,16,2]{1,2,0:T(2,128)}, u32[]{:S(2)}) copy-start(s32[4,16,2]{1,2,0:T(2,128)} %param.27) | copy-start | bytes 1540
  328.2 11.8 %copy-start.4 = (bf16[4096,8]{0,1:T(8,128)(2,1)S(1)}, bf16[4096,8]{0,1:T(8,128)(2,1)}, u32[]{:S(2)}) copy-start(bf16[4096,8]{0,1:T(8,128)(2,1)} %param.20) | copy-start | bytes 196612
  337.3 71.9 %all-reduce.8.cloned.1.call-start = ((), (), s32[]{:S(2)}) async-start(), calls=%async_computation.4 | async-start | bytes 262144 | tf_op jit(solution)/shard_map/psum | solution.py:77
Sparse Core Ops, SparseCore 0:
  11.2 56.9 all-reduce.3
  203.5 27.6 all-gather.4
  248.5 34.3 all-reduce.5
  337.4 34.9 reduce-scatter.1
  374.7 34.4 all-reduce.7
where the time goes:
time: 424 us; the launch traced here: 418 us
  matrix products  139 us (33%)
  local copies, waits for them, and re-layouts  115 us (27%)
  waiting for transfers between devices  73.4 us (17%)
  blocking collectives  42.2 us (10%)
  other arithmetic  33.4 us (8%)
  between operations  14.3 us (3%)
    reshape x1, local copies, waits for them, and re-layouts, body(): in_flat = expert_in.reshape(experts_local, MODEL_WIDTH, 2 * ff_local)  54.3 us
    dot_general x2, matrix products, body(): jnp.einsum('pg,pqd->gqd', group_float, slot_vector * rescale[:, :, None],...  40 us
    dot_general x2, matrix products, body(): jnp.einsum('ptq,ptd->pqd', weights.astype(jnp.bfloat16), value_matrix, pr...  38.3 us
    psum x2, waiting for transfers between devices, head_total(): return lax.psum(partial_value, 'kv')  34.9 us
    dot_general x2, matrix products, body(): jnp.einsum('ptd,pqd->ptq', key_matrix, query_slots, preferred_element_typ...  33.3 us
    reduce_scatter x1, waiting for transfers between devices, body(): lax.psum_scatter(down_part, 'blk', scatter_dimension=1, tiled=True)  32.1 us
    all_gather x2, blocking collectives, joined(): pieces = jax.tree.map(lambda part: lax.all_gather(part, axis), value)  17.9 us
    gather x2, local copies, waits for them, and re-layouts, body(): query_slots = query_groups[group_here]  16.8 us
  transfers between devices with their start and end apart: 5, of which 3 were waited for; matrix products, arithmetic and copies ran while one was open for 26% of the time, Pallas kernels for 0%

commit v1 on v0

--- a/solution.py
+++ b/solution.py
@@ -1,8 +1,11 @@
+import functools
 import math
 
 import jax
 import jax.numpy as jnp
 from jax import lax
+from jax.experimental import pallas as pl
+from jax.experimental.pallas import tpu as pltpu
 from jax.sharding import PartitionSpec as P
 
 MODEL_WIDTH = 4096
@@ -309,7 +312,643 @@
     return layer_out.reshape(DECODE_STEPS, BEAM_TOTAL, width_local)
 
 
+MASKED = -3e38
+CHUNK = 8
+DEPTH = 6
+MESH_IDS = pl.DeviceIdType.MESH
+
+
+def dot32(left, right):
+    return jnp.dot(left, right, preferred_element_type=jnp.float32)
+
+
+def dot32_t(left, right):
+    return lax.dot_general(left, right, (((1,), (1,)), ((), ())), preferred_element_type=jnp.float32)
+
+
+def spread_matrix():
+    rows = lax.broadcasted_iota(jnp.int32, (256, 512), 0)
+    columns = lax.broadcasted_iota(jnp.int32, (256, 512), 1)
+    return jnp.where(columns == 2 * rows, 1.0, 0.0).astype(jnp.bfloat16)
+
+
+def spread(values, matrix, target, start):
+    for piece in range(values.shape[1] // 256):
+        even = dot32(values[:, piece * 256 : piece * 256 + 256], matrix)
+        odd = pltpu.roll(even, 1, 1)
+        first = start + piece * 512
+        target[0:64, first : first + 512] = even.astype(jnp.bfloat16)
+        target[64:128, first : first + 512] = odd.astype(jnp.bfloat16)
+
+
+def greet(parts):
+    barrier = pltpu.get_barrier_semaphore()
+    count = 0
+    for axis, size in parts:
+        me = lax.axis_index(axis)
+        for off in range(1, size):
+            pl.semaphore_signal(
+                barrier,
+                inc=1,
+                device_id={axis: lax.rem(me + off, size)},
+                device_id_type=MESH_IDS,
+            )
+            count += 1
+    pl.semaphore_wait(barrier, count)
+
+
+def push(source, target, send, receive, axis, peer):
+    copy = pltpu.make_async_remote_copy(
+        src_ref=source,
+        dst_ref=target,
+        send_sem=send,
+        recv_sem=receive,
+        device_id={axis: peer},
+        device_id_type=MESH_IDS,
+    )
+    copy.start()
+    return copy
+
+
+def project_kernel(
+    blk_size, x_ref, gain_ref, w_ref, cos_ref, sin_ref, out_ref, wide, part, got, send1, recv1, send2, recv2
+):
+    me = lax.axis_index("blk")
+    greet((("blk", blk_size),))
+    flat = x_ref[...].astype(jnp.float32)
+    pre = (flat * gain_ref[...].astype(jnp.float32)).astype(jnp.bfloat16)
+    spread(pre, spread_matrix(), wide, 0)
+    squares = jnp.broadcast_to(jnp.sum(flat * flat, axis=1, keepdims=True), (64, HEAD_WIDTH))
+    squares = jnp.concatenate([squares, squares], axis=0)
+    high = squares.astype(jnp.bfloat16)
+    part[6] = high
+    part[7] = (squares - high.astype(jnp.float32)).astype(jnp.bfloat16)
+    lhs = wide[...]
+    for c in range(0, 6, 2):
+        right = jnp.concatenate(
+            [w_ref.at[c].reshape(1024, 128)[...], w_ref.at[c + 1].reshape(1024, 128)[...]], axis=1
+        )
+        both = dot32(lhs, right).astype(jnp.bfloat16)
+        part[c] = both[:, :128]
+        part[c + 1] = both[:, 128:]
+
+    def rows_of(index):
+        start = lax.rem(index, 2) * 64 + (index // 2) * 16
+        return pl.ds(pl.multiple_of(start, 16), 16)
+
+    copies = []
+    for off in range(1, blk_size):
+        peer = lax.rem(me + off, blk_size)
+        copies.append(
+            push(part.at[:, rows_of(peer)], got.at[off - 1], send1.at[off - 1], recv1.at[off - 1], "blk", peer)
+        )
+    total = part[:, rows_of(me)].astype(jnp.float32)
+    for off in range(1, blk_size):
+        copies[off - 1].wait_recv()
+        total = total + got[off - 1].astype(jnp.float32)
+    inverse = lax.rsqrt((total[6] + total[7]) * (1.0 / MODEL_WIDTH) + NORM_FLOOR)
+    token_rows = pl.ds(pl.multiple_of((me // 2) * 16, 16), 16)
+    cosine = cos_ref[token_rows, :]
+    sine_part = sin_ref[token_rows, :]
+    for c in range(6):
+        value = total[c] * inverse
+        if c < 5:
+            value = value * cosine + pltpu.roll(value, 64, 1) * sine_part
+        out_ref[me, c] = value.astype(jnp.bfloat16)
+    later = []
+    for off in range(1, blk_size):
+        peer = lax.rem(me + off, blk_size)
+        later.append(
+            push(out_ref.at[me], out_ref.at[me], send2.at[off - 1], recv2.at[off - 1], "blk", peer)
+        )
+    for off in range(1, blk_size):
+        later[off - 1].wait_recv()
+    for off in range(1, blk_size):
+        copies[off - 1].wait_send()
+        later[off - 1].wait_send()
+
+
+def attend_kernel(
+    list_ref, count_ref, qkv_ref, anchor_ref, recent_ref, cache, acc_ref, ml_ref, q, m, l, acc, ring, sems
+):
+    scale = 1.0 / math.sqrt(HEAD_WIDTH)
+    first_chunks = (count_ref[0] + CHUNK - 1) // CHUNK
+    chunks = first_chunks + (count_ref[1] + CHUNK - 1) // CHUNK
+
+    def place(index):
+        group = (index >= first_chunks).astype(jnp.int32)
+        return group, group * 256 + (index - group * first_chunks) * CHUNK
+
+    def fetch(index):
+        slot = lax.rem(index, DEPTH)
+        group, base = place(index)
+        for b in range(CHUNK):
+            block = list_ref[base + b] & 255
+            pltpu.make_async_copy(cache.at[block], ring.at[slot, b], sems.at[slot, b]).start()
+
+    for index in range(DEPTH - 1):
+
+        @pl.when(index < chunks)
+        def _():
+            fetch(jnp.int32(index))
+
+    for group in range(2):
+        for head in range(2):
+            gh = group * 2 + head
+            rows = []
+            for step in range(4):
+                for c in range(4):
+                    rows.append(
+                        qkv_ref[step * 2 + head, c].astype(jnp.float32)[group * 8 : group * 8 + 8]
+                    )
+            query = jnp.concatenate(rows, axis=0).astype(jnp.bfloat16)
+            q[gh] = query
+            empty = jnp.zeros((64, HEAD_WIDTH), jnp.bfloat16)
+            keys = jnp.concatenate([qkv_ref[step * 2 + head, 4] for step in range(4)] + [empty], axis=0)
+            values = jnp.concatenate([qkv_ref[step * 2 + head, 5] for step in range(4)] + [empty], axis=0)
+            score = jnp.where(recent_ref[group] > 0, dot32_t(query, keys), MASKED)
+            top = jnp.maximum(jnp.max(score, axis=1, keepdims=True), NEG_FILL)
+            weight = jnp.exp((score - top) * scale)
+            m[gh] = jnp.broadcast_to(top, (128, 128))
+            l[gh] = weight
+            acc[gh] = dot32(weight.astype(jnp.bfloat16), values)
+
+    lane = lax.broadcasted_iota(jnp.int32, (128, 128), 1)
+
+    def step_body(index, carry):
+        @pl.when(index + DEPTH - 1 < chunks)
+        def _():
+            fetch(index + DEPTH - 1)
+
+        slot = lax.rem(index, DEPTH)
+        group, base = place(index)
+        for b in range(CHUNK):
+            pltpu.make_async_copy(cache.at[0], ring.at[slot, b], sems.at[slot, b]).wait()
+        anchors = anchor_ref[group]
+        allowed = []
+        for b in range(CHUNK):
+            entry = list_ref[base + b]
+            owner = (entry >> 8) & 31
+            limit = entry >> 13
+            allowed.append(lane < jnp.where(anchors == owner, limit, 0))
+        for head in range(2):
+            gh = group * 2 + head
+            query = q[gh]
+            keys = ring[slot, :, 0, head].reshape(CHUNK * 128, 128)
+            scores = dot32_t(query, keys)
+            masked = [
+                jnp.where(allowed[b], scores[:, b * 128 : b * 128 + 128], MASKED) for b in range(CHUNK)
+            ]
+            top = functools.reduce(jnp.maximum, masked)
+            old = m[gh]
+            new = jnp.maximum(old, jnp.max(top, axis=1, keepdims=True))
+            decay = jnp.exp((old - new) * scale)
+            weights = [jnp.exp((part - new) * scale) for part in masked]
+            m[gh] = new
+            l[gh] = l[gh] * decay + functools.reduce(jnp.add, weights)
+            spread_weights = jnp.concatenate([w.astype(jnp.bfloat16) for w in weights], axis=1)
+            values = ring[slot, :, 1, head].reshape(CHUNK * 128, 128)
+            acc[gh] = acc[gh] * decay + dot32(spread_weights, values)
+        return carry
+
+    lax.fori_loop(0, chunks, step_body, 0)
+    for gh in range(4):
+        total = jnp.broadcast_to(jnp.sum(l[gh], axis=1, keepdims=True), (128, 128))
+        ml_ref[gh, 0:8] = jnp.transpose(m[gh])[0:8] * scale
+        ml_ref[gh, 8:16] = jnp.transpose(total)[0:8]
+        result = acc[gh].astype(jnp.bfloat16)
+        acc_ref[gh * 2] = result[:64]
+        acc_ref[gh * 2 + 1] = result[64:]
+
+
+def layer_kernel(
+    blk_size,
+    kv_size,
+    acc_ref,
+    ml_ref,
+    x_ref,
+    wo_ref,
+    gain_ref,
+    router_ref,
+    routes_ref,
+    w_in,
+    w_down,
+    out_ref,
+    inbuf,
+    downbuf,
+    wide,
+    hidden,
+    got_acc,
+    got_ml,
+    coef,
+    attended,
+    opart,
+    got_o,
+    resid,
+    gathered,
+    dpart,
+    got_d,
+    fpart,
+    got_f,
+    outs,
+    in_sem,
+    down_sem,
+    s_acc,
+    r_acc,
+    s_ml,
+    r_ml,
+    s_att,
+    r_att,
+    s_o,
+    r_o,
+    s_res,
+    r_res,
+    s_all,
+    r_all,
+    s_d,
+    r_d,
+    s_f,
+    r_f,
+    s_out,
+    r_out,
+):
+    me = lax.axis_index("blk")
+    my_kv = lax.axis_index("kv")
+    width = out_ref.shape[1]
+
+    def in_copy(tile):
+        return pltpu.make_async_copy(w_in.at[tile // 8, :, lax.rem(tile, 8)], inbuf.at[tile], in_sem.at[tile])
+
+    def down_copy(piece):
+        columns = pl.ds(pl.multiple_of(piece * width, width), width)
+        return pltpu.make_async_copy(w_down.at[:, columns], downbuf.at[piece], down_sem.at[piece])
+
+    lax.fori_loop(0, 16, lambda tile, c: (in_copy(tile).start(), c)[1], 0)
+    lax.fori_loop(0, blk_size, lambda piece, c: (down_copy(piece).start(), c)[1], 0)
+    greet((("blk", blk_size), ("kv", kv_size)))
+
+    waits = []
+    pairs = []
+    for off in range(1, blk_size):
+        peer = lax.rem(me + off, blk_size)
+        one = push(acc_ref.at[peer], got_acc.at[off - 1], s_acc.at[off - 1], r_acc.at[off - 1], "blk", peer)
+        two = push(ml_ref.at[peer // 2], got_ml.at[off - 1], s_ml.at[off - 1], r_ml.at[off - 1], "blk", peer)
+        pairs.append((one, two))
+        waits += [one, two]
+    stats = [ml_ref[me // 2]]
+    for off in range(1, blk_size):
+        pairs[off - 1][1].wait_recv()
+        stats.append(got_ml[off - 1])
+    tops = [stat[0:8] for stat in stats]
+    best = functools.reduce(jnp.maximum, tops)
+    factors = [jnp.exp(top - best) for top in tops]
+    total = functools.reduce(jnp.add, [f * stat[8:16] for f, stat in zip(factors, stats)])
+    rows = jnp.concatenate([(f / total)[0:1] for f in factors], axis=0)
+    coef[...] = jnp.transpose(jnp.concatenate([rows] * 16, axis=0))
+    mine = coef[pl.ds(pl.multiple_of(lax.rem(me, 2) * 64, 64), 64), :]
+    joint = mine[:, 0:1] * acc_ref[me].astype(jnp.float32)
+    for off in range(1, blk_size):
+        pairs[off - 1][0].wait_recv()
+        joint = joint + mine[:, off : off + 1] * got_acc[off - 1].astype(jnp.float32)
+    attended[me] = joint.astype(jnp.bfloat16)
+    copies = []
+    for off in range(1, blk_size):
+        peer = lax.rem(me + off, blk_size)
+        copies.append(
+            push(attended.at[me], attended.at[me], s_att.at[off - 1], r_att.at[off - 1], "blk", peer)
+        )
+    for copy in copies:
+        copy.wait_recv()
+    waits += copies
+
+    heads = []
+    for head in range(2):
+        blocks = [
+            attended[(group * 2 + head) * 2 + half].astype(jnp.float32)
+            for half in range(2)
+            for group in range(2)
+        ]
+        for c in range(4):
+            rows = []
+            for step in range(4):
+                for group in range(2):
+                    block = blocks[(step // 2) * 2 + group]
+                    start = ((step % 2) * 4 + c) * 8
+                    rows.append(block[start : start + 8])
+            heads.append(jnp.concatenate(rows, axis=0).astype(jnp.bfloat16))
+    opart[...] = dot32(jnp.concatenate(heads, axis=1), wo_ref[...]).astype(jnp.bfloat16)
+
+    def step_rows(index):
+        return pl.ds(pl.multiple_of(index * 16, 16), 16)
+
+    copies = []
+    for off in range(1, kv_size):
+        peer = lax.rem(my_kv + off, kv_size)
+        copies.append(
+            push(opart.at[step_rows(peer)], got_o.at[off - 1], s_o.at[off - 1], r_o.at[off - 1], "kv", peer)
+        )
+    sums = x_ref[step_rows(my_kv), :].astype(jnp.float32) + opart[step_rows(my_kv), :].astype(jnp.float32)
+    for off in range(1, kv_size):
+        copies[off - 1].wait_recv()
+        sums = sums + got_o[off - 1].astype(jnp.float32)
+    waits += copies
+    resid[step_rows(my_kv), :] = sums.astype(jnp.bfloat16)
+    copies = []
+    for off in range(1, kv_size):
+        peer = lax.rem(my_kv + off, kv_size)
+        copies.append(
+            push(
+                resid.at[step_rows(my_kv)], resid.at[step_rows(my_kv)], s_res.at[off - 1], r_res.at[off - 1], "kv", peer
+            )
+        )
+    for copy in copies:
+        copy.wait_recv()
+    waits += copies
+
+    gathered[me] = resid[...]
+    core = lax.rem(me, 2)
+    partner = me + 1 - 2 * core
+    chips = blk_size // 2
+    near = push(gathered.at[me], gathered.at[me], s_all.at[0], r_all.at[0], "blk", partner)
+    far = []
+    for off in range(1, chips):
+        peer = lax.rem(me + 2 * off, blk_size)
+        far.append(push(gathered.at[me], gathered.at[me], s_all.at[off], r_all.at[off], "blk", peer))
+    relays = []
+    for off in range(1, chips):
+        far[off - 1].wait_recv()
+        origin = lax.rem(me + blk_size - 2 * off, blk_size)
+        relays.append(
+            push(
+                gathered.at[origin],
+                gathered.at[origin],
+                s_all.at[chips - 1 + off],
+                r_all.at[chips - 1 + off],
+                "blk",
+                partner,
+            )
+        )
+    near.wait_recv()
+    for copy in relays:
+        copy.wait_recv()
+    waits += [near] + far + relays
+
+    matrix = spread_matrix()
+    squares = jnp.zeros((64, 1), jnp.float32)
+    logits = jnp.zeros((64, EXPERTS), jnp.float32)
+    for source in range(blk_size):
+        values = gathered[source].astype(jnp.float32)
+        squares = squares + jnp.sum(values * values, axis=1, keepdims=True)
+        first = source * width
+        pre = (values * gain_ref[:, first : first + width].astype(jnp.float32)).astype(jnp.bfloat16)
+        logits = logits + dot32_t(pre, router_ref[:, first : first + width])
+        spread(pre, matrix, wide, 2 * first)
+    inverse = lax.rsqrt(squares * (1.0 / MODEL_WIDTH) + NORM_FLOOR)
+    logits = logits * inverse
+    lane = lax.broadcasted_iota(jnp.int32, (64, EXPERTS), 1)
+    pick_one = routes_ref[:, 0:1]
+    pick_two = routes_ref[:, 1:2]
+    logit_one = jnp.sum(jnp.where(lane == pick_one, logits, 0.0), axis=1, keepdims=True)
+    logit_two = jnp.sum(jnp.where(lane == pick_two, logits, 0.0), axis=1, keepdims=True)
+    share_one = 1.0 / (1.0 + jnp.exp(logit_two - logit_one))
+    share_two = 1.0 / (1.0 + jnp.exp(logit_one - logit_two))
+    named = []
+    shares = []
+    for local in range(2):
+        expert = my_kv * 2 + local
+        is_one = pick_one == expert
+        is_two = pick_two == expert
+        named.append(jnp.where(is_one | is_two, 1, 0))
+        shares.append(jnp.where(is_one, share_one, jnp.where(is_two, share_two, 0.0)))
+
+    for local in range(2):
+
+        def expert_body(pair, carry, local=local):
+            tile = local * 8 + pair * 2
+            in_copy(tile).wait()
+            in_copy(tile + 1).wait()
+            right = jnp.concatenate(
+                [inbuf.at[tile].reshape(8192, 128)[...], inbuf.at[tile + 1].reshape(8192, 128)[...]], axis=1
+            )
+            both = dot32(wide[...], right)
+            gate = both[:64] * inverse
+            up = both[64:] * inverse
+            act = gate / (1.0 + jnp.exp(-gate)) * up * shares[local]
+            act = jnp.where(named[local] > 0, act, 0.0)
+            hidden[:, pl.ds(pl.multiple_of(local * 1024 + pair * 256, 256), 256)] = act.astype(jnp.bfloat16)
+            return carry
+
+        lax.fori_loop(0, 4, expert_body, 0)
+
+    copies = []
+    mixed = None
+    for off in range(1, blk_size + 1):
+        peer = lax.rem(me + off, blk_size)
+        down_copy(peer).wait()
+        piece = dot32(hidden[...], downbuf[peer])
+        if off < blk_size:
+            dpart[off - 1] = piece.astype(jnp.bfloat16)
+            copies.append(
+                push(dpart.at[off - 1], got_d.at[off - 1], s_d.at[off - 1], r_d.at[off - 1], "blk", peer)
+            )
+        else:
+            mixed = piece
+    for off in range(1, blk_size):
+        copies[off - 1].wait_recv()
+        mixed = mixed + got_d[off - 1].astype(jnp.float32)
+    waits += copies
+    fpart[...] = mixed.astype(jnp.bfloat16)
+    copies = []
+    for off in range(1, kv_size):
+        peer = lax.rem(my_kv + off, kv_size)
+        copies.append(
+            push(fpart.at[step_rows(peer)], got_f.at[off - 1], s_f.at[off - 1], r_f.at[off - 1], "kv", peer)
+        )
+    sums = resid[step_rows(my_kv), :].astype(jnp.float32) + fpart[step_rows(my_kv), :].astype(jnp.float32)
+    for off in range(1, kv_size):
+        copies[off - 1].wait_recv()
+        sums = sums + got_f[off - 1].astype(jnp.float32)
+    waits += copies
+    outs[step_rows(my_kv), :] = sums.astype(jnp.bfloat16)
+    copies = []
+    for off in range(1, kv_size):
+        peer = lax.rem(my_kv + off, kv_size)
+        copies.append(
+            push(
+                outs.at[step_rows(my_kv)], outs.at[step_rows(my_kv)], s_out.at[off - 1], r_out.at[off - 1], "kv", peer
+            )
+        )
+    for copy in copies:
+        copy.wait_recv()
+    waits += copies
+    out_ref[...] = outs[...]
+    for copy in waits:
+        copy.wait_send()
+
+
+def lookup(table, index):
+    slots = jnp.arange(table.shape[0], dtype=jnp.int32)
+    return jnp.sum(jnp.where(index[..., None] == slots, table, 0), axis=-1)
+
+
+def kernel_body(
+    blk_size,
+    kv_size,
+    hidden_in,
+    attn_gain,
+    ffn_gain,
+    query_key_value_weight,
+    out_weight,
+    router_weight,
+    expert_in,
+    expert_down,
+    kv_cache,
+    lengths,
+    tables,
+    parents,
+    routes,
+):
+    bf16, f32 = jnp.bfloat16, jnp.float32
+    vmem = pl.BlockSpec(memory_space=pltpu.VMEM)
+    smem = pl.BlockSpec(memory_space=pltpu.SMEM)
+    hbm = pl.BlockSpec(memory_space=pl.ANY)
+    dma = pltpu.SemaphoreType.DMA
+    width = hidden_in.shape[2]
+    x = hidden_in.reshape(64, width)
+    half = HEAD_WIDTH // 2
+    frequency = ROPE_BASE ** (-(jnp.arange(half, dtype=f32) * (2.0 / HEAD_WIDTH)))
+    token = jnp.arange(64, dtype=jnp.int32)
+    position = jnp.where((token % 16) < BEAM_W, lengths[0], lengths[1]) + token // 16
+    angle = position.astype(f32)[:, None] * frequency
+    cosine, sine_part = jnp.cos(angle), jnp.sin(angle)
+    cosine = jnp.concatenate([cosine, cosine], axis=1)
+    sine_part = jnp.concatenate([-sine_part, sine_part], axis=1)
+    w_qkv = query_key_value_weight.reshape(width, 2, 6, 128).transpose(2, 0, 1, 3)
+    qkv = pl.pallas_call(
+        functools.partial(project_kernel, blk_size),
+        out_shape=jax.ShapeDtypeStruct((blk_size, 6, 16, 128), bf16),
+        in_specs=[vmem] * 5,
+        out_specs=vmem,
+        scratch_shapes=[
+            pltpu.VMEM((128, 2 * width), bf16),
+            pltpu.VMEM((8, 128, 128), bf16),
+            pltpu.VMEM((blk_size - 1, 8, 16, 128), bf16),
+        ]
+        + [dma((blk_size - 1,))] * 4,
+        compiler_params=pltpu.CompilerParams(
+            collective_id=0, has_side_effects=True, vmem_limit_bytes=24 * 2**20
+        ),
+        name="project",
+    )(x, attn_gain.reshape(1, width), w_qkv, cosine, sine_part)
+
+    steps = jnp.arange(DECODE_STEPS, dtype=jnp.int32)
+    current = jnp.broadcast_to(jnp.arange(BEAM_TOTAL, dtype=jnp.int32), (DECODE_STEPS, BEAM_TOTAL))
+    chain = [None] * DECODE_STEPS
+    for k in range(DECODE_STEPS - 1, -1, -1):
+        chain[k] = jnp.where(steps[:, None] >= k, current, -1)
+        current = jnp.where(steps[:, None] >= k, lookup(parents[k], current), current)
+    anchor = current
+    chain = jnp.stack(chain, axis=1)
+    by_group = jnp.moveaxis(anchor.reshape(DECODE_STEPS, 2, BEAM_W), 1, 0)
+    anchor_rows = jnp.broadcast_to(by_group[:, :, None, :, None], (2, 4, 4, BEAM_W, 128)).reshape(2, 128, 128)
+    seen = chain[:, :, :, None] == jnp.arange(BEAM_TOTAL, dtype=jnp.int32)
+    seen = jnp.transpose(seen, (0, 2, 1, 3)).reshape(DECODE_STEPS, 2, BEAM_W, 64)
+    seen = (seen & (lax.axis_index("blk") == 0)).astype(jnp.int32)
+    seen = jnp.pad(jnp.moveaxis(seen, 1, 0), ((0, 0), (0, 0), (0, 0), (0, 64)))
+    recent = jnp.broadcast_to(seen[:, :, None], (2, 4, 4, BEAM_W, 128)).reshape(2, 128, 128)
+
+    slot_count = kv_cache.shape[0]
+    slots = jnp.arange(slot_count, dtype=jnp.int32)
+    flat = tables.reshape(-1)
+    entries = jnp.arange(flat.shape[0], dtype=jnp.int32)
+    here = (slots + lax.axis_index("blk") * slot_count)[:, None] == flat[None, :]
+    entry = jnp.sum(jnp.where(here, entries[None, :], 0), axis=1)
+    owner = entry // BEAM_BLOCKS
+    start = (entry % BEAM_BLOCKS) * BLOCK_POSITIONS
+    group = owner // BEAM_W
+    limit = jnp.clip(jnp.where(group == 0, lengths[0], lengths[1]) - start, 0, BLOCK_POSITIONS)
+    used = jnp.any(owner[:, None] == anchor.reshape(1, -1), axis=1)
+    live = (limit > 0) & used
+    packed = slots + owner * 256 + limit * 8192
+    member = live[None, :] & (group[None, :] == jnp.arange(2, dtype=jnp.int32)[:, None])
+    before = jnp.sum(member[:, None, :] & (slots[None, :] < slots[:, None])[None], axis=2, dtype=jnp.int32)
+    chosen = member[:, None, :] & (before[:, None, :] == slots[None, :, None])
+    listing = jnp.sum(jnp.where(chosen, packed[None, None, :], 0), axis=2).reshape(-1)
+    counts = jnp.sum(member, axis=1, dtype=jnp.int32)
+
+    acc, stats = pl.pallas_call(
+        attend_kernel,
+        out_shape=(jax.ShapeDtypeStruct((8, 64, 128), bf16), jax.ShapeDtypeStruct((4, 16, 128), f32)),
+        in_specs=[smem, smem, vmem, vmem, vmem, hbm],
+        out_specs=(vmem, vmem),
+        scratch_shapes=[
+            pltpu.VMEM((4, 128, 128), bf16),
+            pltpu.VMEM((4, 128, 128), f32),
+            pltpu.VMEM((4, 128, 128), f32),
+            pltpu.VMEM((4, 128, 128), f32),
+            pltpu.VMEM((DEPTH, CHUNK, 2, 2, 128, 128), bf16),
+            dma((DEPTH, CHUNK)),
+        ],
+        compiler_params=pltpu.CompilerParams(vmem_limit_bytes=32 * 2**20),
+        name="attend",
+    )(listing, counts, qkv, anchor_rows, recent, kv_cache)
+
+    w_in = expert_in.reshape(2, MODEL_WIDTH, 2, 8, 128).transpose(0, 1, 3, 2, 4)
+    b, k = blk_size - 1, kv_size - 1
+    out = pl.pallas_call(
+        functools.partial(layer_kernel, blk_size, kv_size),
+        out_shape=jax.ShapeDtypeStruct((64, width), bf16),
+        in_specs=[vmem] * 7 + [hbm] * 2,
+        out_specs=vmem,
+        scratch_shapes=[
+            pltpu.VMEM((16, MODEL_WIDTH, 2, 128), bf16),
+            pltpu.VMEM((blk_size, 2048, width), bf16),
+            pltpu.VMEM((128, 2 * MODEL_WIDTH), bf16),
+            pltpu.VMEM((64, 2048), bf16),
+            pltpu.VMEM((b, 64, 128), bf16),
+            pltpu.VMEM((b, 16, 128), f32),
+            pltpu.VMEM((128, 128), f32),
+            pltpu.VMEM((blk_size, 64, 128), bf16),
+            pltpu.VMEM((64, width), bf16),
+            pltpu.VMEM((k, 16, width), bf16),
+            pltpu.VMEM((64, width), bf16),
+            pltpu.VMEM((blk_size, 64, width), bf16),
+            pltpu.VMEM((b, 64, width), bf16),
+            pltpu.VMEM((b, 64, width), bf16),
+            pltpu.VMEM((64, width), bf16),
+            pltpu.VMEM((k, 16, width), bf16),
+            pltpu.VMEM((64, width), bf16),
+            dma((16,)),
+            dma((blk_size,)),
+        ]
+        + [dma((b,))] * 6
+        + [dma((k,))] * 4
+        + [dma((b,))] * 4
+        + [dma((k,))] * 4,
+        compiler_params=pltpu.CompilerParams(
+            collective_id=1, has_side_effects=True, vmem_limit_bytes=60 * 2**20
+        ),
+        name="layer",
+    )(
+        acc,
+        stats,
+        x,
+        out_weight,
+        ffn_gain.reshape(1, MODEL_WIDTH),
+        router_weight.T,
+        routes.reshape(64, 2),
+        w_in,
+        expert_down.reshape(2048, MODEL_WIDTH),
+    )
+    return out.reshape(DECODE_STEPS, BEAM_TOTAL, width)
+
+
 def solution(mesh):
+    blk_size, kv_size = mesh.shape["blk"], mesh.shape["kv"]
+    if (blk_size, kv_size) == (8, 4):
+        run = functools.partial(kernel_body, blk_size, kv_size)
+    else:
+        run = body
     placed = (
         P(None, None, "blk"),
         P("blk"),
@@ -326,5 +965,5 @@
         P(),
     )
     return jax.shard_map(
-        body, mesh=mesh, in_specs=placed, out_specs=P(None, None, "blk"), check_vma=False
-    )
+        run, mesh=mesh, in_specs=placed, out_specs=P(None, None, "blk"), check_vma=False
+    )

time: 424 us -> 109 us (0.26); the launches traced: 418 us -> 108 us
  matrix products: 139 us -> 0 us
  local copies, waits for them, and re-layouts: 115 us -> 12.5 us
  Pallas kernels: 0 us -> 89.1 us
  waiting for transfers between devices: 73.4 us -> 0 us
  blocking collectives: 42.2 us -> 0 us
  other arithmetic: 33.4 us -> 5.84 us
  between operations: 14.3 us -> 0.22 us
    dot_general x18 -> x0, matrix products: 139 us -> none  [the longest x2 40 us: body(): jnp.einsum('pg,pqd->gqd', group_float, slot_vector * rescale[:, :, None],...]
    pallas_call x0 -> x3, Pallas kernels: none -> 89.1 us  [the longest x1 61.9 us: kernel_body(): pl.pallas_call(functools.partial(layer_kernel, blk_size, kv_size), out_sh...]
    reshape x17 -> x4, local copies, waits for them, and re-layouts: 55.9 us -> 3.17 us  [the longest x1 1.17 us: kernel_body(): query_key_value_weight.reshape(width, 2, 6, 128).transpose(2, 0, 1, 3)]
    psum x3 -> x0, waiting for transfers between devices: 41.2 us -> none  [the longest x2 34.9 us: head_total(): return lax.psum(partial_value, 'kv')]
    reduce_scatter x1 -> x0, waiting for transfers between devices: 32.1 us -> none  [body(): lax.psum_scatter(down_part, 'blk', scatter_dimension=1, tiled=True)]
    gather x17 -> x0, local copies, waits for them, and re-layouts: 27.7 us -> none  [the longest x2 16.8 us: body(): query_slots = query_groups[group_here]]
    all_gather x3 -> x0, blocking collectives: 27.1 us -> none  [the longest x2 17.9 us: joined(): pieces = jax.tree.map(lambda part: lax.all_gather(part, axis), value)]
    scatter x5 -> x0, local copies, waits for them, and re-layouts: 20.3 us -> none  [the longest x1 8.05 us: body(): owner_all = jnp.zeros((BEAM_TOTAL * BEAM_BLOCKS,), jnp.int32).at[tables.r...]
  transfers between devices with their start and end apart: 5 -> 0, of which waited for: 3 -> 0; matrix products, arithmetic and copies ran while one was open for 26% -> 0% of each run, Pallas kernels for 0% -> 0%
where the time goes in v1:
time: 109 us; the launch traced here: 108 us
  Pallas kernels  89.1 us (82%)
  local copies, waits for them, and re-layouts  12.5 us (11%)
  other arithmetic  5.84 us (5%)
    pallas_call x1, Pallas kernels, kernel_body(): pl.pallas_call(functools.partial(layer_kernel, blk_size, kv_size), out_sh...  61.9 us
    pallas_call x1, Pallas kernels, kernel_body(): pl.pallas_call(functools.partial(project_kernel, blk_size), out_shape=jax...  13.7 us
    pallas_call x1, Pallas kernels, kernel_body(): pl.pallas_call(attend_kernel, out_shape=(jax.ShapeDtypeStruct((8, 64, 128...  13.5 us
    unnamed x13, local copies, waits for them, and re-layouts  6.32 us

profile of v1, /device:TPU:0, one launch (start us, length us, event | category | flops | bytes accessed | tf_op | source)
XLA Modules:
  0.0 107.7 jit_solution(9172827771796158952)
XLA Ops:
  0.0 1.1 %select_reduce_fusion = s32[256]{0:T(256)S(1)} fusion(s32[2048]{0:T(1024)} %bitcast.59, s32[256]{0:T(256)S(1)} %iota_add_fusion), kind=kLoop, calls=%fused_computation | loop fusion | flops 1572608 | bytes 10240 | tf_op jit(solution)/shard_map/reduce_sum | solution.py:865
  1.1 0.8 slice_bitcast_fusion.3
  2.0 0.1 select_reduce_fusion.5
  2.1 0.1 iota_select_fusion.1
  2.2 0.2 select_reduce_fusion.4
  2.4 0.1 broadcast_select_fusion.1
  2.5 0.2 select_reduce_fusion.3
  2.7 0.1 broadcast_select_fusion.2
  2.8 0.2 select_reduce_fusion.2
  3.0 0.1 eq.165
  3.1 0.1 compare_reduce_fusion
  3.2 1.4 %fusion.9 = (s32[1]{0:T(128)}, s32[1]{0:T(128)}) fusion(s32[2]{0:T(128)} %param.22), kind=kLoop, calls=%fused_computation.67 | loop fusion | bytes 16 | tf_op jit(solution)/shard_map/slice | solution.py:869
  4.6 1.4 %compare_and_fusion.1 = (pred[256]{0:T(512)(128)(4,1)S(1)}, s32[256]{0:T(256)S(1)}, s32[256]{0:T(256)S(1)}) fusion(pred[256]{0:T(512)(128)(4,1)S(1)} %compare_reduce_fusion, s32[256]{0:T(256)S(1)} %select_reduce_fusion, s32[]{:T(128)} %bitcast.2, s32[]{:T(128)} %bitcast.1), kind=kLoop, calls=%fused_computation.33 | loop fusion | flops 10496 | bytes 3592 | tf_op jit(solution)/shard_map/and | solution.py:871
  6.0 0.1 convert_reduce_fusion.1
  6.1 0.1 convert_reduce_fusion
  6.3 0.2 select_reduce_fusion.1
  6.5 0.7 reshape.622.gain_ref
  7.2 3.6 %copy.25 = bf16[512,2,768]{0,2,1:T(8,128)(2,1)S(1)} copy(bf16[512,2,768]{2,1,0:T(2,128)(2,1)} %param.16) | data formatting | bytes 3145728 | tf_op args[3]
  10.7 0.0 copy-start
  10.8 1.2 %copy.26 = bf16[512,2,6,128]{3,1,0,2:T(2,128)(2,1)S(1)} copy(bf16[512,2,6,128]{0,3,2,1:T(8,128)(2,1)S(1)} %bitcast.54) | data formatting | bytes 3145728 | tf_op jit(solution)/shard_map/reshape | solution.py:826
  11.9 1.3 %fusion.7 = f32[64]{0:T(128)S(1)} fusion(s32[]{:T(128)} %bitcast.2, s32[]{:T(128)} %bitcast.1), kind=kLoop, calls=%fused_computation.56 | loop fusion | flops 1024 | bytes 264 | tf_op jit(solution)/shard_map/convert_element_type | solution.py:822
  13.3 0.2 fusion.1
  13.5 0.1 pad_maximum_fusion
  13.6 0.0 copy-done
  13.6 13.7 %project.1.qkv_ref = bf16[8,6,16,128]{3,2,1,0:T(8,128)(2,1)S(1)} custom-call(bf16[64,512]{1,0:T(8,128)(2,1)S(1)} %bitcast.50, bf16[1,512]{1,0:T(2,128)(2,1)S(1)} %reshape.622.gain_ref, bf16[6,512,2,128]{3,2,1,0:T(2,128)(2,1)S(1)} %bitcast.47, f32[64,128]{1,0:T(8,128)S(1)} %get-tuple-element.27.cos_ref, f32[64,128]{1,0:T(8,128)S(1)} %get-tuple-element.28.sin_ref), custom_call_target="tpu_custom_call" | custom-call | tf_op jit(solution)/shard_map/project/pallas_call | solution.py:827
  27.3 0.1 reduce_sum.88
  27.4 0.1 broadcast_in_dim.189
  27.5 0.1 broadcast_in_dim.190.anchor_ref
  27.6 0.1 bitcast_select_fusion.2
  27.7 0.1 copy.28
  27.8 0.1 eq.175
  27.9 0.1 eq.176
  28.1 0.1 eq.178
  28.2 0.0 copy-start.3
  28.2 0.0 copy-start.4
  28.2 13.5 %attend.1 = (bf16[8,64,128]{2,1,0:T(8,128)(2,1)S(1)}, f32[4,16,128]{2,1,0:T(8,128)S(1)}) custom-call(s32[512]{0:T(512)S(1)} %bitcast.51, s32[2]{0:T(128)S(1)} %get-tuple-element.9.count_ref, bf16[8,6,16,128]{3,2,1,0:T(8,128)(2,1)S(1)} %project.1.qkv_ref, s32[2,128,128]{2,1,0:T(8,128)S(1)} %broadcast_in_dim.190.anchor_ref, s32[2,128,128]{2,1,0:T(8,128)S(1)} %bitcast.48, ...), custom_call_target="tpu_custom_call" | custom-call | tf_op jit(solution)/shard_map/attend/pallas_call | solution.py:879
  41.7 0.0 copy-start.1
  41.7 0.6 copy-done.1
  42.3 0.0 copy-start.2
  42.3 0.6 copy-done.2
  43.0 0.0 copy-done.3
  43.0 0.6 reshape.625.gain_ref
  43.6 0.0 copy-done.4
  43.6 0.7 copy.32
  44.3 61.9 %layer.1 = bf16[64,512]{1,0:T(8,128)(2,1)} custom-call(bf16[8,64,128]{2,1,0:T(8,128)(2,1)} %copy-done.1, f32[4,16,128]{2,1,0:T(8,128)} %copy-done.2, bf16[64,512]{1,0:T(8,128)(2,1)} %bitcast.49, bf16[1024,512]{1,0:T(8,128)(2,1)} %wo_ref.1, bf16[1,4096]{1,0:T(2,128)(2,1)} %reshape.625.gain_ref, bf16[8,4096]{1,0:T(8,128)(2,1)} %bitcast.57, s32[64,2]{1,0:T(8,128)} %bitcast.56, ...), custom_call_target="tpu_custom_call" | custom-call | tf_op jit(solution)/shard_map/layer/pallas_call | solution.py:898
  106.2 1.5 %copy.36 = bf16[4,16,512]{2,1,0:T(8,128)(2,1)} copy(bf16[4,16,512]{2,1,0:T(8,128)(2,1)} %bitcast.55) | data formatting | bytes 131072
  (16 shorter events, 0.1 us)
Async XLA Ops:
  10.7 2.8 %copy-start = (bf16[4,16,512]{2,1,0:T(8,128)(2,1)S(1)}, bf16[4,16,512]{2,1,0:T(8,128)(2,1)}, u32[]{:S(2)}) copy-start(bf16[4,16,512]{2,1,0:T(8,128)(2,1)} %param.13) | copy-start | bytes 196612
  28.2 14.8 %copy-start.3 = (bf16[4096]{0:T(1024)(128)(2,1)S(1)}, bf16[4096]{0:T(1024)(128)(2,1)}, u32[]{:S(2)}) copy-start(bf16[4096]{0:T(1024)(128)(2,1)} %param.15) | copy-start | bytes 24580
  28.2 15.4 %copy-start.4 = (s32[4,16,2]{1,2,0:T(2,128)S(1)}, s32[4,16,2]{1,2,0:T(2,128)}, u32[]{:S(2)}) copy-start(s32[4,16,2]{1,2,0:T(2,128)} %param.25) | copy-start | bytes 1540
  41.7 0.6 copy-start.1
  42.3 0.6 copy-start.2

commit v2 on v1

--- a/solution.py
+++ b/solution.py
@@ -371,9 +371,12 @@
 
 
 def project_kernel(
-    blk_size, x_ref, gain_ref, w_ref, cos_ref, sin_ref, out_ref, wide, part, got, send1, recv1, send2, recv2
+    blk_size, x_ref, gain_ref, cos_ref, sin_ref, w_hbm, out_ref, w_ref, wide, part, got, w_sem, send1, recv1, send2, recv2
 ):
     me = lax.axis_index("blk")
+    loads = [pltpu.make_async_copy(w_hbm.at[:, c], w_ref.at[c], w_sem.at[c]) for c in range(6)]
+    for load in loads:
+        load.start()
     greet((("blk", blk_size),))
     flat = x_ref[...].astype(jnp.float32)
     pre = (flat * gain_ref[...].astype(jnp.float32)).astype(jnp.bfloat16)
@@ -385,6 +388,8 @@
     part[7] = (squares - high.astype(jnp.float32)).astype(jnp.bfloat16)
     lhs = wide[...]
     for c in range(0, 6, 2):
+        loads[c].wait()
+        loads[c + 1].wait()
         right = jnp.concatenate(
             [w_ref.at[c].reshape(1024, 128)[...], w_ref.at[c + 1].reshape(1024, 128)[...]], axis=1
         )
@@ -432,6 +437,7 @@
     list_ref, count_ref, qkv_ref, anchor_ref, recent_ref, cache, acc_ref, ml_ref, q, m, l, acc, ring, sems
 ):
     scale = 1.0 / math.sqrt(HEAD_WIDTH)
+    scale2 = scale * math.log2(math.e)
     first_chunks = (count_ref[0] + CHUNK - 1) // CHUNK
     chunks = first_chunks + (count_ref[1] + CHUNK - 1) // CHUNK
 
@@ -491,24 +497,29 @@
             owner = (entry >> 8) & 31
             limit = entry >> 13
             allowed.append(lane < jnp.where(anchors == owner, limit, 0))
+        held = [(m[group * 2 + h], l[group * 2 + h], acc[group * 2 + h]) for h in range(2)]
+        scores = [
+            dot32_t(q[group * 2 + h], ring[slot, :, 0, h].reshape(CHUNK * 128, 128)) for h in range(2)
+        ]
+        fresh = []
         for head in range(2):
-            gh = group * 2 + head
-            query = q[gh]
-            keys = ring[slot, :, 0, head].reshape(CHUNK * 128, 128)
-            scores = dot32_t(query, keys)
+            old, old_sum, old_acc = held[head]
             masked = [
-                jnp.where(allowed[b], scores[:, b * 128 : b * 128 + 128], MASKED) for b in range(CHUNK)
+                jnp.where(allowed[b], scores[head][:, b * 128 : b * 128 + 128], MASKED)
+                for b in range(CHUNK)
             ]
             top = functools.reduce(jnp.maximum, masked)
-            old = m[gh]
             new = jnp.maximum(old, jnp.max(top, axis=1, keepdims=True))
-            decay = jnp.exp((old - new) * scale)
-            weights = [jnp.exp((part - new) * scale) for part in masked]
-            m[gh] = new
-            l[gh] = l[gh] * decay + functools.reduce(jnp.add, weights)
+            decay = jnp.exp2((old - new) * scale2)
+            weights = [jnp.exp2((part - new) * scale2) for part in masked]
+            new_sum = old_sum * decay + functools.reduce(jnp.add, weights)
             spread_weights = jnp.concatenate([w.astype(jnp.bfloat16) for w in weights], axis=1)
             values = ring[slot, :, 1, head].reshape(CHUNK * 128, 128)
-            acc[gh] = acc[gh] * decay + dot32(spread_weights, values)
+            fresh.append((new, new_sum, old_acc * decay + dot32(spread_weights, values)))
+        for head in range(2):
+            m[group * 2 + head] = fresh[head][0]
+            l[group * 2 + head] = fresh[head][1]
+            acc[group * 2 + head] = fresh[head][2]
         return carry
 
     lax.fori_loop(0, chunks, step_body, 0)
@@ -551,6 +562,9 @@
     fpart,
     got_f,
     outs,
+    sums_in,
+    stat_rows,
+    logit_rows,
     in_sem,
     down_sem,
     s_acc,
@@ -675,7 +689,41 @@
         peer = lax.rem(me + 2 * off, blk_size)
         far.append(push(gathered.at[me], gathered.at[me], s_all.at[off], r_all.at[off], "blk", peer))
     relays = []
-    for off in range(1, chips):
+    matrix = spread_matrix()
+    stat_rows[...] = jnp.zeros_like(stat_rows)
+    logit_rows[...] = jnp.zeros_like(logit_rows)
+
+    def absorb(source, first):
+        values = gathered[source].astype(jnp.float32)
+        stat_rows[...] += jnp.broadcast_to(jnp.sum(values * values, axis=1, keepdims=True), (64, 128))
+        columns = pl.ds(pl.multiple_of(source * width, width), width)
+        pre = (values * gain_ref[:, columns].astype(jnp.float32)).astype(jnp.bfloat16)
+        logit_rows[...] += dot32_t(pre, router_ref[:, columns])
+        spread(pre, matrix, wide, 0)
+        rows = pl.ds(pl.multiple_of(source * width, width), width)
+
+        def tile_body(pair, carry):
+            tile = pair * 2
+            if first:
+                in_copy(tile).wait()
+                in_copy(tile + 1).wait()
+            right = jnp.concatenate(
+                [
+                    inbuf.at[tile, rows].reshape(2 * width, 128)[...],
+                    inbuf.at[tile + 1, rows].reshape(2 * width, 128)[...],
+                ],
+                axis=1,
+            )
+            both = dot32(wide[...], right)
+            if first:
+                sums_in[pair] = both
+            else:
+                sums_in[pair] += both
+            return carry
+
+        lax.fori_loop(0, 8, tile_body, 0)
+
+    def relay(off):
         far[off - 1].wait_recv()
         origin = lax.rem(me + blk_size - 2 * off, blk_size)
         relays.append(
@@ -688,23 +736,21 @@
                 partner,
             )
         )
+        return origin
+
+    absorb(me, True)
     near.wait_recv()
-    for copy in relays:
-        copy.wait_recv()
+    origins = [relay(off) for off in range(1, chips)]
+    absorb(partner, False)
+    for origin in origins:
+        absorb(origin, False)
+    for off in range(1, chips):
+        relays[off - 1].wait_recv()
+        absorb(lax.rem(partner + blk_size - 2 * off, blk_size), False)
     waits += [near] + far + relays
 
-    matrix = spread_matrix()
-    squares = jnp.zeros((64, 1), jnp.float32)
-    logits = jnp.zeros((64, EXPERTS), jnp.float32)
-    for source in range(blk_size):
-        values = gathered[source].astype(jnp.float32)
-        squares = squares + jnp.sum(values * values, axis=1, keepdims=True)
-        first = source * width
-        pre = (values * gain_ref[:, first : first + width].astype(jnp.float32)).astype(jnp.bfloat16)
-        logits = logits + dot32_t(pre, router_ref[:, first : first + width])
-        spread(pre, matrix, wide, 2 * first)
-    inverse = lax.rsqrt(squares * (1.0 / MODEL_WIDTH) + NORM_FLOOR)
-    logits = logits * inverse
+    inverse = lax.rsqrt(stat_rows[:, 0:1] * (1.0 / MODEL_WIDTH) + NORM_FLOOR)
+    logits = logit_rows[...] * inverse
     lane = lax.broadcasted_iota(jnp.int32, (64, EXPERTS), 1)
     pick_one = routes_ref[:, 0:1]
     pick_two = routes_ref[:, 1:2]
@@ -724,13 +770,7 @@
     for local in range(2):
 
         def expert_body(pair, carry, local=local):
-            tile = local * 8 + pair * 2
-            in_copy(tile).wait()
-            in_copy(tile + 1).wait()
-            right = jnp.concatenate(
-                [inbuf.at[tile].reshape(8192, 128)[...], inbuf.at[tile + 1].reshape(8192, 128)[...]], axis=1
-            )
-            both = dot32(wide[...], right)
+            both = sums_in[local * 4 + pair]
             gate = both[:64] * inverse
             up = both[64:] * inverse
             act = gate / (1.0 + jnp.exp(-gate)) * up * shares[local]
@@ -818,28 +858,30 @@
     half = HEAD_WIDTH // 2
     frequency = ROPE_BASE ** (-(jnp.arange(half, dtype=f32) * (2.0 / HEAD_WIDTH)))
     token = jnp.arange(64, dtype=jnp.int32)
-    position = jnp.where((token % 16) < BEAM_W, lengths[0], lengths[1]) + token // 16
+    position = lookup(lengths, (token % 16) // BEAM_W) + token // 16
     angle = position.astype(f32)[:, None] * frequency
     cosine, sine_part = jnp.cos(angle), jnp.sin(angle)
     cosine = jnp.concatenate([cosine, cosine], axis=1)
     sine_part = jnp.concatenate([-sine_part, sine_part], axis=1)
-    w_qkv = query_key_value_weight.reshape(width, 2, 6, 128).transpose(2, 0, 1, 3)
+    w_qkv = query_key_value_weight.reshape(width, 2, 6, 128).transpose(0, 2, 1, 3)
     qkv = pl.pallas_call(
         functools.partial(project_kernel, blk_size),
         out_shape=jax.ShapeDtypeStruct((blk_size, 6, 16, 128), bf16),
-        in_specs=[vmem] * 5,
+        in_specs=[vmem] * 4 + [hbm],
         out_specs=vmem,
         scratch_shapes=[
+            pltpu.VMEM((6, width, 2, 128), bf16),
             pltpu.VMEM((128, 2 * width), bf16),
             pltpu.VMEM((8, 128, 128), bf16),
             pltpu.VMEM((blk_size - 1, 8, 16, 128), bf16),
+            dma((6,)),
         ]
         + [dma((blk_size - 1,))] * 4,
         compiler_params=pltpu.CompilerParams(
             collective_id=0, has_side_effects=True, vmem_limit_bytes=24 * 2**20
         ),
         name="project",
-    )(x, attn_gain.reshape(1, width), w_qkv, cosine, sine_part)
+    )(x, attn_gain.reshape(1, width), cosine, sine_part, w_qkv)
 
     steps = jnp.arange(DECODE_STEPS, dtype=jnp.int32)
     current = jnp.broadcast_to(jnp.arange(BEAM_TOTAL, dtype=jnp.int32), (DECODE_STEPS, BEAM_TOTAL))
@@ -866,7 +908,7 @@
     owner = entry // BEAM_BLOCKS
     start = (entry % BEAM_BLOCKS) * BLOCK_POSITIONS
     group = owner // BEAM_W
-    limit = jnp.clip(jnp.where(group == 0, lengths[0], lengths[1]) - start, 0, BLOCK_POSITIONS)
+    limit = jnp.clip(lookup(lengths, group) - start, 0, BLOCK_POSITIONS)
     used = jnp.any(owner[:, None] == anchor.reshape(1, -1), axis=1)
     live = (limit > 0) & used
     packed = slots + owner * 256 + limit * 8192
@@ -903,7 +945,7 @@
         scratch_shapes=[
             pltpu.VMEM((16, MODEL_WIDTH, 2, 128), bf16),
             pltpu.VMEM((blk_size, 2048, width), bf16),
-            pltpu.VMEM((128, 2 * MODEL_WIDTH), bf16),
+            pltpu.VMEM((128, 2 * width), bf16),
             pltpu.VMEM((64, 2048), bf16),
             pltpu.VMEM((b, 64, 128), bf16),
             pltpu.VMEM((b, 16, 128), f32),
@@ -918,6 +960,9 @@
             pltpu.VMEM((64, width), bf16),
             pltpu.VMEM((k, 16, width), bf16),
             pltpu.VMEM((64, width), bf16),
+            pltpu.VMEM((8, 128, 256), f32),
+            pltpu.VMEM((64, 128), f32),
+            pltpu.VMEM((64, EXPERTS), f32),
             dma((16,)),
             dma((blk_size,)),
         ]

time: 109 us -> 112 us (1.028); the launches traced: 108 us -> 114 us
  Pallas kernels: 89.1 us -> 100 us
  local copies, waits for them, and re-layouts: 12.5 us -> 8.63 us
  other arithmetic: 5.84 us -> 4.65 us
    pallas_call x1, Pallas kernels: 61.9 us -> 67.4 us  [kernel_body(): pl.pallas_call(functools.partial(layer_kernel, blk_size, kv_size), out_sh...]
    pallas_call x1, Pallas kernels: 13.5 us -> 17.5 us  [kernel_body(): pl.pallas_call(attend_kernel, out_shape=(jax.ShapeDtypeStruct((8, 64, 128...]
    pallas_call x1, Pallas kernels: 13.7 us -> 15.3 us  [kernel_body(): pl.pallas_call(functools.partial(project_kernel, blk_size), out_shape=jax...]
    reduce_sum x4 -> x6, other arithmetic: 0.8 us -> 2.28 us  [lookup(): return jnp.sum(jnp.where(index[..., None] == slots, table, 0), axis=-1)]
    slice x1 -> x0, local copies, waits for them, and re-layouts: 1.39 us -> none  [kernel_body(): lengths[0]]
    unnamed x13 -> x14, local copies, waits for them, and re-layouts: 6.32 us -> 4.98 us
    and x1, other arithmetic: 1.36 us -> 0.02 us  [kernel_body(): live = (limit > 0) & used]
    convert_element_type x1, other arithmetic: 1.34 us -> 0.01 us  [kernel_body(): angle = position.astype(f32)[:, None] * frequency]
where the time goes in v2:
time: 112 us; the launch traced here: 114 us
  Pallas kernels  100 us (89%)
  local copies, waits for them, and re-layouts  8.63 us (8%)
  other arithmetic  4.65 us (4%)
    pallas_call x1, Pallas kernels, kernel_body(): pl.pallas_call(functools.partial(layer_kernel, blk_size, kv_size), out_sh...  67.4 us
    pallas_call x1, Pallas kernels, kernel_body(): pl.pallas_call(attend_kernel, out_shape=(jax.ShapeDtypeStruct((8, 64, 128...  17.5 us
    pallas_call x1, Pallas kernels, kernel_body(): pl.pallas_call(functools.partial(project_kernel, blk_size), out_shape=jax...  15.3 us
    unnamed x14, local copies, waits for them, and re-layouts  4.98 us
    reduce_sum x6, other arithmetic, lookup(): return jnp.sum(jnp.where(index[..., None] == slots, table, 0), axis=-1)  2.28 us

profile of v2, /device:TPU:0, one launch (start us, length us, event | category | flops | bytes accessed | tf_op | source)
XLA Modules:
  0.0 113.6 jit_solution(18269334996868140841)
XLA Ops:
  0.0 0.8 slice_bitcast_fusion.3
  0.8 0.1 select_reduce_fusion.5
  1.0 0.1 iota_select_fusion.1
  1.1 0.2 select_reduce_fusion.4
  1.3 0.1 broadcast_select_fusion.1
  1.4 0.2 select_reduce_fusion.3
  1.6 0.1 bitcast_select_fusion.2
  1.7 0.1 copy.24
  1.8 0.1 eq.195
  1.9 0.1 eq.196
  2.1 0.1 eq.198
  2.2 0.1 broadcast_select_fusion.2
  2.3 0.2 select_reduce_fusion.2
  2.5 0.1 eq.182
  2.6 1.1 select_reduce_fusion
  3.7 0.1 compare_reduce_fusion
  3.8 0.7 fusion.2
  4.6 0.1 convert_reduce_fusion.1
  4.7 0.1 convert_reduce_fusion
  4.9 0.2 select_reduce_fusion.1
  5.1 0.1 reduce_sum.108
  5.2 0.1 broadcast_in_dim.193
  5.3 0.1 broadcast_in_dim.194.anchor_ref
  5.4 0.7 fusion.6
  6.1 0.2 fusion.1
  6.4 0.1 pad_maximum_fusion
  6.4 0.7 reshape.641.gain_ref
  7.1 0.0 copy-start
  7.1 1.4 %copy-done = bf16[512,2,768]{2,1,0:T(2,128)(2,1)S(1)} copy-done((bf16[512,2,768]{2,1,0:T(2,128)(2,1)S(1)}, bf16[512,2,768]{2,1,0:T(2,128)(2,1)}, u32[]{:S(2)}) %copy-start) | copy-done | bytes 1572888
  8.5 0.0 copy-start.1
  8.5 0.8 copy-done.1
  9.4 15.3 %project.1.qkv_ref = bf16[8,6,16,128]{3,2,1,0:T(8,128)(2,1)S(1)} custom-call(bf16[64,512]{1,0:T(8,128)(2,1)S(1)} %bitcast.49, bf16[1,512]{1,0:T(2,128)(2,1)S(1)} %reshape.641.gain_ref, f32[64,128]{1,0:T(8,128)S(1)} %get-tuple-element.26.cos_ref, f32[64,128]{1,0:T(8,128)S(1)} %get-tuple-element.27.sin_ref, bf16[512,6,2,128]{3,2,1,0:T(2,128)(2,1)S(1)} %bitcast.46), custom_call_target="tpu_custom_call" | custom-call | tf_op jit(solution)/shard_map/project/pallas_call | solution.py:867
  24.7 0.0 copy-start.5
  24.7 0.0 copy-start.4
  24.7 17.5 %attend.1 = (bf16[8,64,128]{2,1,0:T(8,128)(2,1)S(1)}, f32[4,16,128]{2,1,0:T(8,128)S(1)}) custom-call(s32[512]{0:T(512)S(1)} %bitcast.50, s32[2]{0:T(128)S(1)} %get-tuple-element.9.count_ref, bf16[8,6,16,128]{3,2,1,0:T(8,128)(2,1)S(1)} %project.1.qkv_ref, s32[2,128,128]{2,1,0:T(8,128)S(1)} %broadcast_in_dim.194.anchor_ref, s32[2,128,128]{2,1,0:T(8,128)S(1)} %bitcast.47, ...), custom_call_target="tpu_custom_call" | custom-call | tf_op jit(solution)/shard_map/attend/pallas_call | solution.py:921
  42.2 0.0 copy-start.2
  42.2 0.6 copy-done.2
  42.9 0.0 copy-start.3
  42.9 0.6 copy-done.3
  43.5 0.0 copy-done.5
  43.5 0.7 copy.28
  44.2 0.0 copy-done.4
  44.2 0.6 reshape.644.gain_ref
  44.8 67.4 %layer.1 = bf16[64,512]{1,0:T(8,128)(2,1)} custom-call(bf16[8,64,128]{2,1,0:T(8,128)(2,1)} %copy-done.2, f32[4,16,128]{2,1,0:T(8,128)} %copy-done.3, bf16[64,512]{1,0:T(8,128)(2,1)} %bitcast.48, bf16[1024,512]{1,0:T(8,128)(2,1)} %wo_ref.1, bf16[1,4096]{1,0:T(2,128)(2,1)} %reshape.644.gain_ref, bf16[8,4096]{1,0:T(8,128)(2,1)} %bitcast.55, s32[64,2]{1,0:T(8,128)} %bitcast.54, ...), custom_call_target="tpu_custom_call" | custom-call | tf_op jit(solution)/shard_map/layer/pallas_call | solution.py:940
  112.2 1.5 %copy.32 = bf16[4,16,512]{2,1,0:T(8,128)(2,1)} copy(bf16[4,16,512]{2,1,0:T(8,128)(2,1)} %bitcast.53) | data formatting | bytes 131072
  (19 shorter events, 0.2 us)
Async XLA Ops:
  7.1 1.4 %copy-start = (bf16[512,2,768]{2,1,0:T(2,128)(2,1)S(1)}, bf16[512,2,768]{2,1,0:T(2,128)(2,1)}, u32[]{:S(2)}) copy-start(bf16[512,2,768]{2,1,0:T(2,128)(2,1)} %param.16) | copy-start | bytes 4718596
  8.5 0.8 copy-start.1
  24.7 18.8 %copy-start.5 = (s32[4,16,2]{1,2,0:T(2,128)S(1)}, s32[4,16,2]{1,2,0:T(2,128)}, u32[]{:S(2)}) copy-start(s32[4,16,2]{1,2,0:T(2,128)} %param.25) | copy-start | bytes 1540
  24.7 19.4 %copy-start.4 = (bf16[4096]{0:T(1024)(128)(2,1)S(1)}, bf16[4096]{0:T(1024)(128)(2,1)}, u32[]{:S(2)}) copy-start(bf16[4096]{0:T(1024)(128)(2,1)} %param.15) | copy-start | bytes 24580
  42.2 0.6 copy-start.2
  42.9 0.6 copy-start.3
